TPU v7x, 512 devices: a whole 4x4x16 slice. The times are simulated.
512 devices in a mesh: dp: 16 (over z_lo, core), seq: 32 (over y, x, z_hi).
Axes of the slice: x: 4, y: 4, z: 16 (z_hi: 2, z_lo: 8; z = z_hi * 8 + z_lo), core: 2. Of those that a mesh axis runs over, the one named last changes fastest.
Arguments:
- queries: bfloat16 [16, 4096, 2048], P('dp', 'seq'), may hold values from -40 to 40, as said below
- keys: bfloat16 [16, 4096, 2048], P('dp', 'seq'), may hold values from -10 to 10, as said below
- values: bfloat16 [16, 4096, 2048], P('dp', 'seq'), may hold values from -6 to 6
- position_keys: bfloat16 [384, 2048], P('dp'), may hold values from -6 to 6
- content_bias: bfloat16 [2048], P('dp'), may hold values from -3 to 3
- position_bias: bfloat16 [2048], P('dp'), may hold values from -3 to 3
- out_grad: bfloat16 [16, 4096, 2048], P('dp', 'seq'), may hold values from -6 to 6
Outputs:
- attended: bfloat16 [16, 4096, 2048], P('dp', 'seq')
- query_grad: bfloat16 [16, 4096, 2048], P('dp', 'seq')
- key_grad: bfloat16 [16, 4096, 2048], P('dp', 'seq')
- value_grad: bfloat16 [16, 4096, 2048], P('dp', 'seq')
- position_key_grad: float32 [384, 2048], P('dp')
- content_grad: float32 [2048], P('dp')
- position_grad: float32 [2048], P('dp')
Inputs may be any that keep to these rules, and one draw needn't show every extreme that they name: `queries`: entries bounded. `keys`: entries bounded.
All inputs are finite; a program needn't handle non-finite values.
Results may differ from a plain program's by a relative error of at most 0.0098.
Values may be sent and summed in bfloat16 or wider, within the bound.
A program may use at most 128 MiB of HBM per device.

v0:
```python
import math

import jax
import jax.numpy as jnp
from jax import lax
from jax.sharding import PartitionSpec as P

H = 16
HEAD = 128
SEG = 128
MEM = 256
HD = 2048
REL = 384


def from_behind(value, axis, by):
    count = lax.axis_size(axis)
    pairs = [(i, i + by) for i in range(count) if 0 <= i + by < count]
    return lax.ppermute(value, axis, pairs)


def skew_left(reversed_scores, seg_rows, rel_cols):
    heads = reversed_scores.shape[0]
    widened = jnp.concatenate(
        [reversed_scores, jnp.zeros((heads, seg_rows, seg_rows), reversed_scores.dtype)], axis=2
    )
    flat = widened.reshape(heads, seg_rows * (rel_cols + seg_rows))
    taken = flat[:, seg_rows - 1 : seg_rows - 1 + seg_rows * (rel_cols + seg_rows - 1)]
    return taken.reshape(heads, seg_rows, rel_cols + seg_rows - 1)[:, :, :rel_cols]


def skew_right(grad_scores, seg_rows, rel_cols):
    heads = grad_scores.shape[0]
    widened = jnp.concatenate(
        [jnp.zeros((heads, seg_rows, seg_rows - 1), grad_scores.dtype), grad_scores], axis=2
    )
    width = rel_cols + seg_rows - 1
    flat = jnp.concatenate(
        [widened.reshape(heads, seg_rows * width), jnp.zeros((heads, seg_rows), grad_scores.dtype)],
        axis=1,
    )
    return flat.reshape(heads, seg_rows, width + 1)[:, :, :rel_cols]


def group_pass(pieces, allowed):
    content_heads, position_heads, key_heads, value_heads, flipped_table, grad_heads = pieces
    factor = HEAD ** (-0.5)
    content_scores = jnp.einsum(
        "ihd,jhd->hij", content_heads, key_heads, preferred_element_type=jnp.float32
    )
    reversed_scores = jnp.einsum(
        "ihd,rhd->hir", position_heads, flipped_table, preferred_element_type=jnp.float32
    )
    positional = skew_left(reversed_scores, SEG, REL)
    scores = (content_scores + positional) * factor
    highest = jnp.max(jnp.where(allowed[None], scores, -1e30), axis=-1, keepdims=True)
    raised = jnp.exp(jnp.where(allowed[None], scores - highest, -1e30))
    weights = raised / jnp.sum(raised, axis=-1, keepdims=True)
    rounded_weights = weights.astype(jnp.bfloat16)
    attended = jnp.einsum(
        "hij,jhd->ihd", rounded_weights, value_heads, preferred_element_type=jnp.float32
    )
    grad_probs = jnp.einsum(
        "ihd,jhd->hij", grad_heads, value_heads, preferred_element_type=jnp.float32
    )
    weighted_mean = jnp.sum(weights * grad_probs, axis=-1, keepdims=True)
    grad_scores = (weights * (grad_probs - weighted_mean) * factor).astype(jnp.bfloat16)
    reversed_grad = skew_right(grad_scores, SEG, REL)
    grad_content = jnp.einsum(
        "hij,jhd->ihd", grad_scores, key_heads, preferred_element_type=jnp.float32
    )
    grad_position = jnp.einsum(
        "hir,rhd->ihd", reversed_grad, flipped_table, preferred_element_type=jnp.float32
    )
    key_part = jnp.einsum(
        "hij,ihd->jhd", grad_scores, content_heads, preferred_element_type=jnp.float32
    )
    value_part = jnp.einsum(
        "hij,ihd->jhd", rounded_weights, grad_heads, preferred_element_type=jnp.float32
    )
    table_reversed = jnp.einsum(
        "hir,ihd->rhd", reversed_grad, position_heads, preferred_element_type=jnp.float32
    )
    return (attended, grad_content, grad_position, key_part, value_part, table_reversed)


def segment_pass(
    query_rows, key_rows, value_rows, grad_rows, table_rows, content_bias, position_bias, segment
):
    group_width = math.gcd(H, 4)
    group_count = H // group_width

    def split_heads(array, rows):
        return array.reshape(rows, group_count, group_width, HEAD).transpose(1, 0, 2, 3)

    def join_heads(array, rows):
        return array.transpose(1, 0, 2, 3).reshape(rows, HD)

    query_float = query_rows.astype(jnp.float32)
    content_query = (query_float + content_bias.astype(jnp.float32)).astype(jnp.bfloat16)
    position_query = (query_float + position_bias.astype(jnp.float32)).astype(jnp.bfloat16)
    query_index = jnp.arange(SEG, dtype=jnp.int32)[:, None]
    column_index = jnp.arange(REL, dtype=jnp.int32)[None, :]
    distance = MEM + query_index - column_index
    allowed = (distance >= 0) & (segment * SEG - MEM + column_index >= 0)
    pieces = (
        split_heads(content_query, SEG),
        split_heads(position_query, SEG),
        split_heads(key_rows, REL),
        split_heads(value_rows, REL),
        split_heads(jnp.flip(table_rows, axis=0), REL),
        split_heads(grad_rows, SEG),
    )
    results = lax.map(lambda group: group_pass(group, allowed), pieces)
    attended = join_heads(results[0], SEG).astype(jnp.bfloat16)
    grad_content = join_heads(results[1], SEG)
    grad_position = join_heads(results[2], SEG)
    query_grad = (grad_content + grad_position).astype(jnp.bfloat16)
    key_part = join_heads(results[3], REL)
    value_part = join_heads(results[4], REL)
    table_grad = jnp.flip(join_heads(results[5], REL), axis=0)
    content_part = jnp.sum(grad_content, axis=0)
    position_part = jnp.sum(grad_position, axis=0)
    return (attended, query_grad, key_part, value_part, table_grad, content_part, position_part)


def local(queries, keys, values, position_keys, content_bias, position_bias, out_grad):
    table_rows, content_full, position_full = (
        lax.all_gather(position_keys, "dp", axis=0, tiled=True),
        lax.all_gather(content_bias, "dp", axis=0, tiled=True),
        lax.all_gather(position_bias, "dp", axis=0, tiled=True),
    )
    segment = lax.axis_index("seq")
    own_keys = keys[0]
    own_values = values[0]
    piece_rows = min(SEG, MEM)
    reach_count = MEM // piece_rows
    earlier = []
    for offset in range(reach_count):
        earlier.append(from_behind((own_keys, own_values), "seq", reach_count - offset))
    key_rows = jnp.concatenate([shifted[0] for shifted in earlier] + [own_keys], axis=0)
    value_rows = jnp.concatenate([shifted[1] for shifted in earlier] + [own_values], axis=0)
    attended, query_grad, key_part, value_part, table_grad, content_part, position_part = (
        segment_pass(
            queries[0],
            key_rows,
            value_rows,
            out_grad[0],
            table_rows,
            content_full,
            position_full,
            segment,
        )
    )
    key_total = key_part[MEM:]
    value_total = value_part[MEM:]
    for offset in range(reach_count):
        got_keys, got_values = from_behind(
            (
                key_part[offset * piece_rows : (offset + 1) * piece_rows],
                value_part[offset * piece_rows : (offset + 1) * piece_rows],
            ),
            "seq",
            offset - reach_count,
        )
        key_total = key_total.at[SEG - piece_rows :].add(got_keys)
        value_total = value_total.at[SEG - piece_rows :].add(got_values)
    summed = lax.psum((table_grad, content_part, position_part), ("dp", "seq"))
    dp_index = lax.axis_index("dp")
    share_rows = REL // lax.axis_size("dp")
    share_columns = HD // lax.axis_size("dp")
    table_share = lax.dynamic_slice_in_dim(summed[0], dp_index * share_rows, share_rows, 0)
    content_share = lax.dynamic_slice_in_dim(summed[1], dp_index * share_columns, share_columns, 0)
    position_share = lax.dynamic_slice_in_dim(summed[2], dp_index * share_columns, share_columns, 0)
    return (
        attended[None],
        query_grad[None],
        key_total.astype(jnp.bfloat16)[None],
        value_total.astype(jnp.bfloat16)[None],
        table_share,
        content_share,
        position_share,
    )


def solution(mesh):
    placed = (
        P("dp", "seq", None),
        P("dp", "seq", None),
        P("dp", "seq", None),
        P("dp", None),
        P("dp"),
        P("dp"),
        P("dp", "seq", None),
    )
    return jax.shard_map(
        local,
        mesh=mesh,
        in_specs=placed,
        out_specs=(
            P("dp", "seq", None),
            P("dp", "seq", None),
            P("dp", "seq", None),
            P("dp", "seq", None),
            P("dp", None),
            P("dp"),
            P("dp"),
        ),
        check_vma=False,
    )
```

profile of v0, /device:TPU:6, one launch (start us, length us, event | category | flops | bytes accessed | tf_op | source)
XLA Modules:
  0.0 953.6 jit_solution(7623443818731116769)
XLA Ops:
  8.0 3.4 collective-permute-start
  11.4 15.7 %collective-permute-start.1 = (bf16[128,2048]{1,0:T(8,128)(2,1)}, bf16[128,2048]{1,0:T(8,128)(2,1)S(1)}, u32[]{:S(2)}, u32[]{:S(2)}) collective-permute-start(bf16[128,2048]{1,0:T(8,128)(2,1)} %bitcast.207), channel_id=1, source_target_pairs={{0,1},{1,2},{2,3},{3,4},{4,5},{5,6},{6,7},{7,8},{8,9},{9,10},{10,1... | collective-permute-start | bytes 1572872 | tf_op jit(solution)/shard_map/ppermute | solution.py:19
  28.4 3.4 collective-permute-start.2
  36.5 112.5 %all-gather.1 = bf16[16,1,128]{2,1,0:T(2,128)(2,1)S(1)} all-gather(bf16[1,1,128]{2,1,0:T(2,128)(2,1)S(1)} %bitcast.213), channel_id=1, replica_groups=mesh['dp'=16,'seq'=32] {'dp'}, dimensions={0}, use_global_device_ids=true | all-gather | bytes 4352 | tf_op jit(solution)/shard_map/all_gather | solution.py:131
  149.0 25.1 %all-gather = bf16[16,1,128]{2,1,0:T(2,128)(2,1)S(1)} all-gather(bf16[1,1,128]{2,1,0:T(2,128)(2,1)S(1)} %bitcast.214), channel_id=1, replica_groups=mesh['dp'=16,'seq'=32] {'dp'}, dimensions={0}, use_global_device_ids=true | all-gather | bytes 4352 | tf_op jit(solution)/shard_map/all_gather | solution.py:130
  177.6 2.6 maximum_bitcast_fusion.1
  183.6 16.9 %rev.8 = bf16[384,2048]{0,1:T(8,128)(2,1)} reverse(bf16[384,2048]{0,1:T(8,128)(2,1)S(1)} %copy.72), dimensions={0} | reverse | bytes 3145728 | tf_op jit(solution)/shard_map/jit(_flip)/rev | solution.py:111
  200.4 116.6 %while.29 = (s32[]{:T(128)}, bf16[4,128,4,128]{1,3,2,0:T(8,128)(2,1)}, f32[4,128,4,128]{1,3,2,0:T(8,128)}, f32[4,128,4,128]{1,3,2,0:T(8,128)}, f32[4,384,4,128]{...) while((s32[]{:T(128)}, ...), condition=%wide.region_4.5_spmd.clone, body=%wide.region_0.4_spmd.clone.sunk | while | flops 460411648 | bytes 39893080 | solution.py:114
  207.6 4.4 fusion.152
  212.0 2.0 fusion.153
  214.0 2.8 fusion.150
  218.6 2.1 fusion.154
  220.6 2.0 fusion.151
  222.7 4.2 fusion.149
  226.9 2.7 fusion.147
  236.8 4.4 fusion.152
  243.1 2.8 fusion.150
  247.7 2.0 fusion.154
  249.8 2.0 fusion.151
  251.8 4.2 fusion.149
  256.0 2.7 fusion.147
  265.9 4.4 fusion.152
  272.2 2.8 fusion.150
  276.8 2.1 fusion.154
  278.9 2.0 fusion.151
  280.9 4.2 fusion.149
  285.2 2.7 fusion.147
  295.0 4.4 fusion.152
  301.4 2.8 fusion.150
  306.0 2.1 fusion.154
  308.0 2.0 fusion.151
  310.1 4.2 fusion.149
  314.3 2.7 fusion.147
  317.0 3.1 fusion.87
  321.5 3.0 collective-permute-start.6
  325.9 8.1 collective-permute-start.7
  334.0 3.2 fusion.88
  338.5 2.8 collective-permute-start.4
  342.7 8.1 collective-permute-start.5
  350.8 2.4 copy.102
  353.2 15.6 %rev.9 = f32[384,2048]{1,0:T(8,128)} reverse(f32[384,2048]{1,0:T(8,128)S(1)} %copy.102), dimensions={0} | reverse | bytes 6291456 | tf_op jit(solution)/shard_map/jit(_flip)/rev | solution.py:121
  370.0 2.5 bitcast_reduce_fusion
  372.6 213.4 %all-reduce.3 = (f32[2048]{0:T(1024)S(1)}, f32[2048]{0:T(1024)S(1)}) all-reduce(f32[2048]{0:T(1024)S(1)} %bitcast.212, f32[2048]{0:T(1024)S(1)} %bitcast.211), channel_id=1, replica_groups=mesh['dp'=16,'seq'=32] {'dp','seq'}, use_global_device_ids=true, to_apply=%region_7.8 | all-reduce | flops 4096 | bytes 32768 | tf_op jit(solution)/shard_map/psum | solution.py:168
  587.8 2.1 copy.95
  589.9 2.0 copy.94
  591.9 2.5 fusion.83
  594.4 2.5 fusion.82
  596.9 348.2 %all-reduce.6.cloned.1.call-done = f32[384,2048]{1,0:T(8,128)} async-done(((f32[384,2048]{1,0:T(8,128)}), f32[384,2048]{1,0:T(8,128)}) %all-reduce.6.cloned.1.call-update) | async-done | bytes 3145744 | tf_op jit(solution)/shard_map/psum | solution.py:168
  (125 shorter events, 64.8 us)
Async XLA Ops:
  7.2 29.3 %copy-start.6 = (bf16[128]{0:T(256)(128)(2,1)S(1)}, bf16[128]{0:T(256)(128)(2,1)}, u32[]{:S(2)}) copy-start(bf16[128]{0:T(256)(128)(2,1)} %param.30) | copy-start | bytes 772
  7.2 141.8 %copy-start.7 = (bf16[128]{0:T(256)(128)(2,1)S(1)}, bf16[128]{0:T(256)(128)(2,1)}, u32[]{:S(2)}) copy-start(bf16[128]{0:T(256)(128)(2,1)} %param.29) | copy-start | bytes 772
  7.2 166.9 %copy-start.5 = (bf16[1,128,2048]{2,1,0:T(8,128)(2,1)S(1)}, bf16[1,128,2048]{2,1,0:T(8,128)(2,1)}, u32[]{:S(2)}) copy-start(bf16[1,128,2048]{2,1,0:T(8,128)(2,1)} %param.31) | copy-start | bytes 1572868
  7.2 174.5 %all-gather.4.cloned.1.call-start = ((), (), s32[]{:S(2)}) async-start(), calls=%async_computation | async-start | bytes 1671168 | tf_op jit(solution)/shard_map/all_gather | solution.py:129
  7.9 937.2 %all-reduce.6.cloned.1.call-start = ((), (), s32[]{:S(2)}) async-start(), calls=%async_computation.1 | async-start | bytes 6291456 | tf_op jit(solution)/shard_map/psum | solution.py:168
  8.0 168.0 %collective-permute-start = (bf16[128,2048]{1,0:T(8,128)(2,1)}, bf16[128,2048]{1,0:T(8,128)(2,1)}, u32[]{:S(2)}, u32[]{:S(2)}) collective-permute-start(bf16[128,2048]{1,0:T(8,128)(2,1)} %bitcast.206), channel_id=1, source_target_pairs={{0,2},{1,3},{2,4},{3,5},{4,6},{5,7},{6,8},{7,9},{8,10},{9,11},{10,... | collective-permute-start | bytes 1572872 | tf_op jit(solution)/shard_map/ppermute | solution.py:19
  11.4 166.0 %collective-permute-start.1 = (bf16[128,2048]{1,0:T(8,128)(2,1)}, bf16[128,2048]{1,0:T(8,128)(2,1)S(1)}, u32[]{:S(2)}, u32[]{:S(2)}) collective-permute-start(bf16[128,2048]{1,0:T(8,128)(2,1)} %bitcast.207), channel_id=1, source_target_pairs={{0,1},{1,2},{2,3},{3,4},{4,5},{5,6},{6,7},{7,8},{8,9},{9,10},{10,1... | collective-permute-start | bytes 1572872 | tf_op jit(solution)/shard_map/ppermute | solution.py:19
  28.4 149.2 %collective-permute-start.2 = (bf16[128,2048]{0,1:T(8,128)(2,1)S(1)}, bf16[128,2048]{0,1:T(8,128)(2,1)}, u32[]{:S(2)}, u32[]{:S(2)}) collective-permute-start(bf16[128,2048]{0,1:T(8,128)(2,1)S(1)} %bitcast.200), channel_id=1, source_target_pairs={{0,2},{1,3},{2,4},{3,5},{4,6},{5,7},{6,8},{7,9},{8,10},{9,11},{10,... | collective-permute-start | bytes 1572872 | tf_op jit(solution)/shard_map/ppermute | solution.py:19
  31.8 145.8 %collective-permute-start.3 = (bf16[128,2048]{0,1:T(8,128)(2,1)S(1)}, bf16[128,2048]{0,1:T(8,128)(2,1)}, u32[]{:S(2)}, u32[]{:S(2)}) collective-permute-start(bf16[128,2048]{0,1:T(8,128)(2,1)S(1)} %bitcast.201), channel_id=1, source_target_pairs={{0,1},{1,2},{2,3},{3,4},{4,5},{5,6},{6,7},{7,8},{8,9},{9,10},{10,1... | collective-permute-start | bytes 1572872 | tf_op jit(solution)/shard_map/ppermute | solution.py:19
  200.4 11.6 %copy-start.2 = (bf16[4,128,4,128]{1,3,2,0:T(8,128)(2,1)}, bf16[4,128,4,128]{1,3,2,0:T(8,128)(2,1)S(1)}, u32[]{:S(2)}) copy-start(bf16[4,128,4,128]{1,3,2,0:T(8,128)(2,1)S(1)} %get-tuple-element.420) | copy-start | bytes 1572868 | tf_op jit(solution)/shard_map/while
  222.7 7.0 copy-start.3
  229.6 11.5 %copy-start.2 = (bf16[4,128,4,128]{1,3,2,0:T(8,128)(2,1)}, bf16[4,128,4,128]{1,3,2,0:T(8,128)(2,1)S(1)}, u32[]{:S(2)}) copy-start(bf16[4,128,4,128]{1,3,2,0:T(8,128)(2,1)S(1)} %get-tuple-element.420) | copy-start | bytes 1572868 | tf_op jit(solution)/shard_map/while
  251.8 7.0 copy-start.3
  258.8 11.5 %copy-start.2 = (bf16[4,128,4,128]{1,3,2,0:T(8,128)(2,1)}, bf16[4,128,4,128]{1,3,2,0:T(8,128)(2,1)S(1)}, u32[]{:S(2)}) copy-start(bf16[4,128,4,128]{1,3,2,0:T(8,128)(2,1)S(1)} %get-tuple-element.420) | copy-start | bytes 1572868 | tf_op jit(solution)/shard_map/while
  280.9 7.0 copy-start.3
  287.9 11.5 %copy-start.2 = (bf16[4,128,4,128]{1,3,2,0:T(8,128)(2,1)}, bf16[4,128,4,128]{1,3,2,0:T(8,128)(2,1)S(1)}, u32[]{:S(2)}) copy-start(bf16[4,128,4,128]{1,3,2,0:T(8,128)(2,1)S(1)} %get-tuple-element.420) | copy-start | bytes 1572868 | tf_op jit(solution)/shard_map/while
  310.1 7.0 copy-start.3
  321.5 270.5 %collective-permute-start.6 = (f32[128,2048]{1,0:T(8,128)}, f32[128,2048]{1,0:T(8,128)}, u32[]{:S(2)}, u32[]{:S(2)}) collective-permute-start(f32[128,2048]{1,0:T(8,128)} %copy.100), channel_id=1, source_target_pairs={{2,0},{3,1},{4,2},{5,3},{6,4},{7,5},{8,6},{9,7},{10,8},{11,9},{12,... | collective-permute-start | bytes 3145736 | tf_op jit(solution)/shard_map/ppermute | solution.py:19
  325.9 266.0 %collective-permute-start.7 = (f32[128,2048]{1,0:T(8,128)}, f32[128,2048]{1,0:T(8,128)}, u32[]{:S(2)}, u32[]{:S(2)}) collective-permute-start(f32[128,2048]{1,0:T(8,128)} %copy.101), channel_id=1, source_target_pairs={{1,0},{2,1},{3,2},{4,3},{5,4},{6,5},{7,6},{8,7},{9,8},{10,9},{11,1... | collective-permute-start | bytes 3145736 | tf_op jit(solution)/shard_map/ppermute | solution.py:19
  338.5 255.9 %collective-permute-start.4 = (f32[128,2048]{1,0:T(8,128)}, f32[128,2048]{1,0:T(8,128)}, u32[]{:S(2)}, u32[]{:S(2)}) collective-permute-start(f32[128,2048]{1,0:T(8,128)} %copy.97), channel_id=1, source_target_pairs={{2,0},{3,1},{4,2},{5,3},{6,4},{7,5},{8,6},{9,7},{10,8},{11,9},{12,... | collective-permute-start | bytes 3145736 | tf_op jit(solution)/shard_map/ppermute | solution.py:19
  342.7 251.8 %collective-permute-start.5 = (f32[128,2048]{1,0:T(8,128)}, f32[128,2048]{1,0:T(8,128)}, u32[]{:S(2)}, u32[]{:S(2)}) collective-permute-start(f32[128,2048]{1,0:T(8,128)} %copy.98), channel_id=1, source_target_pairs={{1,0},{2,1},{3,2},{4,3},{5,4},{6,5},{7,6},{8,7},{9,8},{10,9},{11,1... | collective-permute-start | bytes 3145736 | tf_op jit(solution)/shard_map/ppermute | solution.py:19
  368.8 1.2 copy-start.4
  368.8 218.3 %copy-start = (f32[128,4,4,128]{0,3,2,1:T(8,128)S(1)}, f32[128,4,4,128]{0,3,2,1:T(8,128)}, u32[]{:S(2)}) copy-start(f32[128,4,4,128]{0,3,2,1:T(8,128)} %get-tuple-element.270) | copy-start | bytes 3145732
  368.8 218.6 %copy-start.1 = (f32[128,4,4,128]{0,3,2,1:T(8,128)S(1)}, f32[128,4,4,128]{0,3,2,1:T(8,128)}, u32[]{:S(2)}) copy-start(f32[128,4,4,128]{0,3,2,1:T(8,128)} %get-tuple-element.273) | copy-start | bytes 3145732
Sparse Core Ops, SparseCore 0:
  10.1 140.9 all-gather.3
  369.0 576.1 all-reduce.5
where the time goes:
time: 955 us; the launch traced here: 954 us
  blocking collectives  351 us (37%)
  waiting for transfers between devices  349 us (37%)
  matrix products  86.6 us (9%)
  local copies, waits for them, and re-layouts  79.8 us (8%)
  starting transfers between devices  46.6 us (5%)
  other arithmetic  25.9 us (3%)
  between operations  14.4 us (2%)
    psum x1, waiting for transfers between devices, local(): summed = lax.psum((table_grad, content_part, position_part), ('dp', 'seq'))  348 us
    psum x1, blocking collectives, local(): summed = lax.psum((table_grad, content_part, position_part), ('dp', 'seq'))  213 us
    all_gather x1, blocking collectives, local(): lax.all_gather(position_bias, 'dp', axis=0, tiled=True)  112 us
    ppermute x8, starting transfers between devices, from_behind(): return lax.ppermute(value, axis, pairs)  46.5 us
    all_gather x1, blocking collectives, local(): lax.all_gather(content_bias, 'dp', axis=0, tiled=True)  25.1 us
  transfers between devices with their start and end apart: 10, of which 1 were waited for; matrix products, arithmetic and copies ran while one was open for 5% of the time, Pallas kernels for 0%

commit v1 on v0

v1 whole, which is shorter than its diff:
```python
import functools

import jax
import jax.numpy as jnp
from jax import lax
from jax.experimental import pallas as pl
from jax.experimental.pallas import tpu as pltpu
from jax.sharding import PartitionSpec as P

H = 16
HEAD = 128
SEG = 128
MEM = 256
HD = 2048
REL = 384
DP = 16
NZ = 8
PLANE = 16
ROWS = REL // DP
MSG = 32
TGRAD = REL + 16
PARTNERS = (PLANE - 1) + (NZ - 1) + 1 + 2

F32 = jnp.float32
BF16 = jnp.bfloat16


def dot_nt(a, b):
    return lax.dot_general(a, b, (((1,), (1,)), ((), ())), preferred_element_type=F32)


def dot_nn(a, b):
    return lax.dot_general(a, b, (((1,), (0,)), ((), ())), preferred_element_type=F32)


def dot_tn(a, b):
    return lax.dot_general(a, b, (((0,), (0,)), ((), ())), preferred_element_type=F32)


def columns(head):
    return pl.ds(pl.multiple_of(head * HEAD, HEAD), HEAD)


def kernel(
    q_hbm, k_hbm, v_hbm, g_hbm, table_ref, ub_ref, vb_ref,
    att_ref, qg_ref, kg_ref, vg_ref, tg_ref, cg_ref, pg_ref,
    q_buf, g_buf, k_buf, v_buf, own_k, own_v, back_k, back_v, got_k, got_v,
    msg_f, tz, flat, table, tgrad_out, tgrad_in, parts, sib_in, half_in, pair_out, pair_in, fin,
    local_sem, own_sem, halo_s, halo_r, ret_s, ret_r, tz_s, tz_r, sib_s, sib_r,
    tab_s, tab_r, tg_s, tg_r, half_s, half_r, pair_s, pair_r, fin_s, fin_r,
):
    dp = lax.axis_index("dp")
    seq = lax.axis_index("seq")
    zl = dp // 2
    core = dp % 2
    other = 1 - core
    plane = seq // 2
    zh = seq % 2

    def remote(src, dst, ss, rs, to_dp, to_seq):
        return pltpu.make_async_remote_copy(
            src_ref=src, dst_ref=dst, send_sem=ss, recv_sem=rs,
            device_id={"dp": to_dp, "seq": to_seq}, device_id_type=pl.DeviceIdType.MESH,
        )

    def seq_at(step):
        return (seq + step + 32) % 32

    def plane_seq(p):
        return p * 2 + zh

    load_q = pltpu.make_async_copy(q_hbm, q_buf, local_sem.at[0])
    load_g = pltpu.make_async_copy(g_hbm, g_buf, local_sem.at[1])

    def load_own(h, which):
        src, dst = ((k_hbm, k_buf), (v_hbm, v_buf))[which]
        return pltpu.make_async_copy(
            src.at[:, columns(h)], dst.at[h, pl.ds(MEM, SEG)], own_sem.at[which, h]
        )

    barrier = pltpu.get_barrier_semaphore()

    def greet(to_dp, to_seq):
        pl.semaphore_signal(
            barrier, inc=1, device_id={"dp": to_dp, "seq": to_seq},
            device_id_type=pl.DeviceIdType.MESH,
        )

    greet(dp, seq_at(1))
    greet(dp, seq_at(-1))
    greet(zl * 2 + other, seq)

    @pl.loop(1, NZ)
    def _(p):
        greet(((zl + p) % NZ) * 2 + core, seq)

    @pl.loop(1, PLANE)
    def _(p):
        greet(dp, plane_seq((plane + p) % PLANE))

    load_q.start()
    load_g.start()

    @pl.loop(0, H)
    def _(h):
        load_own(h, 0).start()
        load_own(h, 1).start()

    rows_in = table_ref[:, columns(plane)].astype(F32)
    for r in range(ROWS):
        msg_f[ROWS - 1 - r : ROWS - r, :] = rows_in[r : r + 1, :]
    msg_f[ROWS : ROWS + 1, :] = ub_ref[...].astype(F32)
    msg_f[ROWS + 1 : ROWS + 2, :] = vb_ref[...].astype(F32)
    msg_f[ROWS + 2 : MSG, :] = jnp.zeros((MSG - ROWS - 2, HEAD), F32)
    tz[core, zl] = msg_f[...].astype(BF16)

    pl.semaphore_wait(barrier, PARTNERS)

    def table_z(target, sem):
        return remote(tz.at[core, zl], tz.at[core, zl], tz_s.at[target], tz_r.at[sem], target * 2 + core, seq)

    @pl.loop(1, NZ)
    def _(p):
        table_z((zl + p) % NZ, zl).start()

    def halo(h, which, step):
        src, dst = ((k_hbm, k_buf), (v_hbm, v_buf))[which]
        return remote(
            src.at[:, columns(h)], dst.at[h, pl.ds(MEM - step * SEG, SEG)],
            halo_s.at[which, step - 1, h], halo_r.at[which, step - 1, h], dp, seq_at(step),
        )

    @pl.loop(0, H)
    def _(h):
        for step in (1, 2):
            for which in (0, 1):
                halo(h, which, step).start()

    @pl.loop(1, NZ)
    def _(p):
        source = (zl + p) % NZ
        remote(tz.at[core, zl], tz.at[core, source], tz_s.at[source], tz_r.at[source], source * 2 + core, seq).wait_recv()

    sib_table = remote(tz.at[core], tz.at[core], sib_s.at[0], sib_r.at[0], zl * 2 + other, seq)
    sib_table.start()
    remote(tz.at[core], tz.at[other], sib_s.at[0], sib_r.at[0], zl * 2 + other, seq).wait_recv()

    for d in range(DP):
        low = REL - ROWS * (d + 1)
        flat[low : low + ROWS, :] = tz[d % 2, d // 2].astype(F32)[:ROWS]
    table[plane] = flat[...].astype(BF16)

    def table_plane(p, slot, target):
        return remote(table.at[plane], table.at[slot], tab_s.at[p], tab_r.at[slot], dp, plane_seq(target))

    @pl.loop(1, PLANE)
    def _(p):
        table_plane(p, plane, (plane + p) % PLANE).start()

    load_q.wait()
    load_g.wait()

    @pl.loop(1, PLANE)
    def _(p):
        source = (plane + p) % PLANE
        table_plane(p, source, source).wait_recv()

    query_index = lax.broadcasted_iota(jnp.int32, (SEG, REL), 0)
    column_index = lax.broadcasted_iota(jnp.int32, (SEG, REL), 1)
    factor = HEAD ** (-0.5)
    mirror = (
        lax.broadcasted_iota(jnp.int32, (SEG, SEG), 0) + lax.broadcasted_iota(jnp.int32, (SEG, SEG), 1) == SEG - 1
    ).astype(F32).astype(BF16)

    def give_back(h, which, step):
        src, dst = ((back_k, got_k), (back_v, got_v))[which]
        rows = pl.ds(MEM - step * SEG, SEG)
        return remote(
            src.at[h, rows], dst.at[h, rows],
            ret_s.at[which, step - 1, h], ret_r.at[which, step - 1, h], dp, seq_at(-step),
        )

    def send_tgrad(h):
        return remote(tgrad_out.at[h], tgrad_in.at[plane], tg_s.at[h], tg_r.at[plane], dp, plane_seq(h))

    @pl.loop(0, H)
    def _(h):
        for which in (0, 1):
            load_own(h, which).wait()
            for step in (1, 2):
                halo(h, which, step).wait_recv()
        at = columns(h)
        query = q_buf[:, at].astype(F32)
        grad = g_buf[:, at]
        biases = tz[h % 2, h // 2].astype(F32)
        content_query = (query + biases[ROWS : ROWS + 1]).astype(BF16)
        position_query = (query + biases[ROWS + 1 : ROWS + 2]).astype(BF16)
        keys = k_buf[h]
        values = v_buf[h]
        rows = table[h]
        positional = pltpu.roll(dot_nt(position_query, rows), REL - SEG + 1, 1, stride=1, stride_axis=0)
        scores = (dot_nt(content_query, keys) + positional) * factor
        allowed = (column_index <= query_index + MEM) & (column_index >= MEM - seq * SEG)
        scores = jnp.where(allowed, scores, -1e30)
        highest = jnp.max(scores, axis=1, keepdims=True)
        raised = jnp.where(allowed, jnp.exp(scores - highest), 0.0)
        weights = raised * (1.0 / jnp.sum(raised, axis=1, keepdims=True))
        rounded = weights.astype(BF16)
        att_ref[:, at] = dot_nn(rounded, values).astype(BF16)
        grad_probs = dot_nt(grad, values)
        mean = jnp.sum(weights * grad_probs, axis=1, keepdims=True)
        grad_scores = (weights * (grad_probs - mean) * factor).astype(BF16)
        backwards = dot_nn(mirror, grad_scores)
        skewed = dot_nn(mirror, pltpu.roll(backwards, 0, 1, stride=1, stride_axis=0).astype(BF16)).astype(BF16)
        grad_content = dot_nn(grad_scores, keys)
        grad_position = dot_nn(skewed, rows)
        qg_ref[:, at] = (grad_content + grad_position).astype(BF16)
        key_part = dot_tn(grad_scores, content_query)
        own_k[h] = key_part[MEM:]
        back_k[h] = key_part[:MEM].astype(BF16)
        value_part = dot_tn(rounded, grad)
        own_v[h] = value_part[MEM:]
        back_v[h] = value_part[:MEM].astype(BF16)
        for step in (1, 2):
            for which in (0, 1):
                give_back(h, which, step).start()
        tgrad_out[h, :REL] = dot_tn(skewed, position_query).astype(BF16)
        content_sum = jnp.sum(grad_content, axis=0, keepdims=True)
        position_sum = jnp.sum(grad_position, axis=0, keepdims=True)
        content_high = content_sum.astype(BF16).astype(F32)
        position_high = position_sum.astype(BF16).astype(F32)
        line = lax.broadcasted_iota(jnp.int32, (TGRAD - REL, HEAD), 0)
        sums = jnp.where(line == 0, content_high, jnp.where(line == 1, content_sum - content_high, jnp.where(
            line == 2, position_high, jnp.where(line == 3, position_sum - position_high, 0.0))))
        tgrad_out[h, REL:] = sums.astype(BF16)

        @pl.when(h != plane)
        def _():
            send_tgrad(h).start()

    flat[...] = tgrad_out[plane, :REL].astype(F32)
    msg_f[0:16, :] = tgrad_out[plane, REL:].astype(F32)

    @pl.loop(1, PLANE)
    def _(p):
        source = (plane + p) % PLANE
        remote(tgrad_out.at[source], tgrad_in.at[source], tg_s.at[source], tg_r.at[source], dp, plane_seq(source)).wait_recv()
        flat[...] += tgrad_in[source, :REL].astype(F32)
        msg_f[0:16, :] += tgrad_in[source, REL:].astype(F32)

    tail_rows = msg_f[0:16, :]
    content_total = tail_rows[0:1] + tail_rows[1:2]
    position_total = tail_rows[2:3] + tail_rows[3:4]
    line = lax.broadcasted_iota(jnp.int32, (MSG - ROWS, HEAD), 0)
    sums = jnp.where(line == 0, content_total, jnp.where(line == 1, position_total, 0.0))
    for d in range(DP):
        low = REL - ROWS * (d + 1)
        parts[d % 2, d // 2, :ROWS] = flat[low : low + ROWS, :]
        parts[d % 2, d // 2, ROWS:] = sums

    sib_parts = remote(parts.at[other], sib_in, sib_s.at[1], sib_r.at[1], zl * 2 + other, seq)
    sib_parts.start()
    sib_parts.wait_recv()
    parts[core] += sib_in[...]

    def send_half(target, slot):
        return remote(parts.at[core, target], half_in.at[slot], half_s.at[target], half_r.at[slot], target * 2 + core, seq)

    @pl.loop(1, NZ)
    def _(p):
        send_half((zl + p) % NZ, zl).start()

    pair_out[...] = parts[core, zl]

    @pl.loop(1, NZ)
    def _(p):
        source = (zl + p) % NZ
        send_half(source, source).wait_recv()
        pair_out[...] += half_in[source]

    pair = remote(pair_out, pair_in, pair_s, pair_r, dp, plane * 2 + 1 - zh)
    pair.start()
    pair.wait_recv()
    fin[plane] = pair_out[...] + pair_in[...]

    def send_fin(p, slot, target):
        return remote(fin.at[plane], fin.at[slot], fin_s.at[p], fin_r.at[slot], dp, plane_seq(target))

    @pl.loop(1, PLANE)
    def _(p):
        send_fin(p, plane, (plane + p) % PLANE).start()

    @pl.loop(1, PLANE)
    def _(p):
        source = (plane + p) % PLANE
        send_fin(p, source, source).wait_recv()

    @pl.loop(0, H)
    def _(h):
        tg_ref[:, columns(h)] = fin[h, :ROWS]

    mine = fin[dp]
    cg_ref[...] = mine[ROWS : ROWS + 1]
    pg_ref[...] = mine[ROWS + 1 : ROWS + 2]

    @pl.loop(0, H)
    def _(h):
        for which in (0, 1):
            for step in (1, 2):
                give_back(h, which, step).wait_recv()
        at = columns(h)
        kg_ref[:, at] = (own_k[h] + got_k[h, :SEG].astype(F32) + got_k[h, SEG:].astype(F32)).astype(BF16)
        vg_ref[:, at] = (own_v[h] + got_v[h, :SEG].astype(F32) + got_v[h, SEG:].astype(F32)).astype(BF16)

    sib_table.wait_send()
    sib_parts.wait_send()
    pair.wait_send()

    @pl.loop(1, NZ)
    def _(p):
        target = (zl + p) % NZ
        table_z(target, zl).wait_send()
        send_half(target, zl).wait_send()

    @pl.loop(1, PLANE)
    def _(p):
        target = (plane + p) % PLANE
        table_plane(p, plane, target).wait_send()
        send_fin(p, plane, target).wait_send()
        send_tgrad(target).wait_send()

    @pl.loop(0, H)
    def _(h):
        for step in (1, 2):
            for which in (0, 1):
                halo(h, which, step).wait_send()
                give_back(h, which, step).wait_send()


def local(queries, keys, values, position_keys, content_bias, position_bias, out_grad):
    any_space = pl.BlockSpec(memory_space=pl.ANY)
    vmem = pl.BlockSpec(memory_space=pltpu.VMEM)
    block = jax.ShapeDtypeStruct((SEG, HD), BF16)
    line = jax.ShapeDtypeStruct((1, HEAD), F32)
    dma = pltpu.SemaphoreType.DMA
    heads = lambda rows, dtype: pltpu.VMEM((H, rows, HEAD), dtype)
    attended, query_grad, key_grad, value_grad, table_grad, content_grad, position_grad = pl.pallas_call(
        kernel,
        out_shape=(block, block, block, block, jax.ShapeDtypeStruct((ROWS, HD), F32), line, line),
        in_specs=[any_space] * 4 + [vmem] * 3,
        out_specs=(vmem,) * 7,
        scratch_shapes=[
            pltpu.VMEM((SEG, HD), BF16),
            pltpu.VMEM((SEG, HD), BF16),
            heads(REL, BF16),
            heads(REL, BF16),
            heads(SEG, F32),
            heads(SEG, F32),
            heads(MEM, BF16),
            heads(MEM, BF16),
            heads(MEM, BF16),
            heads(MEM, BF16),
            pltpu.VMEM((MSG, HEAD), F32),
            pltpu.VMEM((2, NZ, MSG, HEAD), BF16),
            pltpu.VMEM((REL, HEAD), F32),
            heads(REL, BF16),
            heads(TGRAD, BF16),
            heads(TGRAD, BF16),
            pltpu.VMEM((2, NZ, MSG, HEAD), F32),
            pltpu.VMEM((NZ, MSG, HEAD), F32),
            pltpu.VMEM((NZ, MSG, HEAD), F32),
            pltpu.VMEM((MSG, HEAD), F32),
            pltpu.VMEM((MSG, HEAD), F32),
            heads(MSG, F32),
            dma((2,)),
            dma((2, H)),
            dma((2, 2, H)),
            dma((2, 2, H)),
            dma((2, 2, H)),
            dma((2, 2, H)),
            dma((NZ,)),
            dma((NZ,)),
            dma((2,)),
            dma((2,)),
            dma((PLANE,)),
            dma((PLANE,)),
            dma((H,)),
            dma((PLANE,)),
            dma((NZ,)),
            dma((NZ,)),
            dma,
            dma,
            dma((PLANE,)),
            dma((PLANE,)),
        ],
        compiler_params=pltpu.CompilerParams(
            collective_id=0, has_side_effects=True, vmem_limit_bytes=48 * 2**20
        ),
    )(
        queries[0], keys[0], values[0], out_grad[0],
        position_keys, content_bias[None], position_bias[None],
    )
    return (
        attended[None],
        query_grad[None],
        key_grad[None],
        value_grad[None],
        jnp.flip(table_grad, axis=0),
        content_grad[0],
        position_grad[0],
    )


def solution(mesh):
    placed = (
        P("dp", "seq", None),
        P("dp", "seq", None),
        P("dp", "seq", None),
        P("dp", None),
        P("dp"),
        P("dp"),
        P("dp", "seq", None),
    )
    return jax.shard_map(
        local,
        mesh=mesh,
        in_specs=placed,
        out_specs=(
            P("dp", "seq", None),
            P("dp", "seq", None),
            P("dp", "seq", None),
            P("dp", "seq", None),
            P("dp", None),
            P("dp"),
            P("dp"),
        ),
        check_vma=False,
    )
```

time: 955 us -> 300 us (0.31)
  blocking collectives: 351 us -> 0 us
  waiting for transfers between devices: 349 us -> 0 us
  Pallas kernels: 0 us -> 283 us
  matrix products: 86.6 us -> 0 us
  local copies, waits for them, and re-layouts: 79.8 us -> 14.8 us
  starting transfers between devices: 46.6 us -> 0 us
  other arithmetic: 25.9 us -> 0 us
  between operations: 14.4 us -> 0.67 us
    psum x1 -> x0, waiting for transfers between devices: 348 us -> none  [local(): summed = lax.psum((table_grad, content_part, position_part), ('dp', 'seq'))]
    pallas_call x0 -> x1, Pallas kernels: none -> 283 us  [local(): pl.pallas_call(kernel, out_shape=(block, block, block, block, jax.ShapeDt...]
    psum x1 -> x0, blocking collectives: 213 us -> none  [local(): summed = lax.psum((table_grad, content_part, position_part), ('dp', 'seq'))]
    all_gather x2 -> x0, blocking collectives: 138 us -> none  [the longest x1 112 us: local(): lax.all_gather(position_bias, 'dp', axis=0, tiled=True)]
    dot_general x36 -> x0, matrix products: 86.6 us -> none  [the longest x4 17.6 us: group_pass(): jnp.einsum('hij,ihd->jhd', grad_scores, content_heads, preferred_element_...]
    ppermute x8 -> x0, starting transfers between devices: 46.5 us -> none  [from_behind(): return lax.ppermute(value, axis, pairs)]
    rev x2 -> x1, local copies, waits for them, and re-layouts: 32.5 us -> 4.86 us  [local(): jnp.flip(table_grad, axis=0)]
    slice x12 -> x0, local copies, waits for them, and re-layouts: 14.7 us -> none  [the longest x3 5.82 us: local(): key_part[offset * piece_rows:(offset + 1) * piece_rows]]
  transfers between devices with their start and end apart: 10 -> 0, of which waited for: 1 -> 0; matrix products, arithmetic and copies ran while one was open for 5% -> 0% of each run, Pallas kernels for 0% -> 0%
where the time goes in v1:
time: 300 us; the launch traced here: 299 us
  Pallas kernels  283 us (94%)
  local copies, waits for them, and re-layouts  14.8 us (5%)
    pallas_call x1, Pallas kernels, local(): pl.pallas_call(kernel, out_shape=(block, block, block, block, jax.ShapeDt...  283 us
    unnamed x20, local copies, waits for them, and re-layouts  9.9 us

profile of v1, /device:TPU:6, one launch (start us, length us, event | category | flops | bytes accessed | tf_op | source)
XLA Modules:
  0.0 298.8 jit_solution(4299159687693673691)
XLA Ops:
  0.6 0.0 copy-start.5
  0.6 0.0 copy-start.6
  0.7 0.6 copy-done.5
  1.3 0.0 copy-done.6
  1.3 0.0 copy-start
  1.3 1.0 copy-done
  2.3 0.0 copy-start.1
  2.4 1.0 copy-done.1
  3.4 0.0 copy-start.2
  3.4 1.0 copy-done.2
  4.4 0.0 copy-start.3
  4.4 1.0 copy-done.3
  5.5 0.0 copy-start.4
  5.5 0.9 copy-done.4
  6.4 283.4 %shard_map.126 = (bf16[128,2048]{1,0:T(8,128)(2,1)S(1)}, bf16[128,2048]{1,0:T(8,128)(2,1)S(1)}, bf16[128,2048]{1,0:T(8,128)(2,1)S(1)}, bf16[128,2048]{1,0:T(8,12...) custom-call(bf16[128,2048]{1,0:T(8,128)(2,1)S(1)} %bitcast.16, ...), custom_call_target="tpu_custom_call" | custom-call | tf_op jit(solution)/shard_map/pallas_call | solution.py:347
  289.7 4.9 %rev.4 = f32[24,2048]{1,0:T(8,128)} reverse(f32[24,2048]{1,0:T(8,128)S(1)} %get-tuple-element.18), dimensions={0} | reverse | bytes 393216 | tf_op jit(solution)/shard_map/jit(_flip)/rev | solution.py:408
  294.6 0.8 copy.20
  295.4 0.8 copy.21
  296.2 0.8 copy.22
  297.0 0.8 copy.23
  297.8 0.5 copy.24
  298.3 0.5 copy.25
Async XLA Ops:
  0.6 0.7 copy-start.5
  0.6 0.7 copy-start.6
  1.3 1.0 copy-start
  2.3 1.0 copy-start.1
  3.4 1.0 copy-start.2
  4.4 1.0 copy-start.3
  5.5 0.9 copy-start.4

commit v2 on v1

--- a/solution.py
+++ b/solution.py
@@ -19,7 +19,10 @@
 ROWS = REL // DP
 MSG = 32
 TGRAD = REL + 16
-PARTNERS = (PLANE - 1) + (NZ - 1) + 1 + 2
+STAT = 3
+STAGES = (1, 6)
+RELEASE = (4, 2)
+PARTNERS = (PLANE - 1) + 2 * (NZ - 1) + 1 + 2
 
 F32 = jnp.float32
 BF16 = jnp.bfloat16
@@ -44,10 +47,10 @@
 def kernel(
     q_hbm, k_hbm, v_hbm, g_hbm, table_ref, ub_ref, vb_ref,
     att_ref, qg_ref, kg_ref, vg_ref, tg_ref, cg_ref, pg_ref,
-    q_buf, g_buf, k_buf, v_buf, own_k, own_v, back_k, back_v, got_k, got_v,
-    msg_f, tz, flat, table, tgrad_out, tgrad_in, parts, sib_in, half_in, pair_out, pair_in, fin,
-    local_sem, own_sem, halo_s, halo_r, ret_s, ret_r, tz_s, tz_r, sib_s, sib_r,
-    tab_s, tab_r, tg_s, tg_r, half_s, half_r, pair_s, pair_r, fin_s, fin_r,
+    q_buf, g_buf, k_buf, v_buf, own_k, own_v, query_in, grad_in, stats, stats_out, stats_in, stats_rows,
+    msg_f, tz, flat, table, tgrad_out, tgrad_in, parts, sib_in, half_out, half_in, fin,
+    local_sem, own_sem, halo_s, halo_r, stat_s, stat_r, tz_s, tz_r, sib_s, sib_r,
+    tab_s, tab_r, tg_s, tg_r, half_s, half_r, fin_s, fin_r,
 ):
     dp = lax.axis_index("dp")
     seq = lax.axis_index("seq")
@@ -69,6 +72,9 @@
     def plane_seq(p):
         return p * 2 + zh
 
+    def turn(i, step):
+        return (i + seq_at(step) // 2) % H
+
     load_q = pltpu.make_async_copy(q_hbm, q_buf, local_sem.at[0])
     load_g = pltpu.make_async_copy(g_hbm, g_buf, local_sem.at[1])
 
@@ -92,7 +98,8 @@
 
     @pl.loop(1, NZ)
     def _(p):
-        greet(((zl + p) % NZ) * 2 + core, seq)
+        for half in (0, 1):
+            greet(((zl + p) % NZ) * 2 + core, plane * 2 + half)
 
     @pl.loop(1, PLANE)
     def _(p):
@@ -102,9 +109,9 @@
     load_g.start()
 
     @pl.loop(0, H)
-    def _(h):
-        load_own(h, 0).start()
-        load_own(h, 1).start()
+    def _(i):
+        load_own(turn(i, 0), 0).start()
+        load_own(turn(i, 0), 1).start()
 
     rows_in = table_ref[:, columns(plane)].astype(F32)
     for r in range(ROWS):
@@ -114,6 +121,8 @@
     msg_f[ROWS + 2 : MSG, :] = jnp.zeros((MSG - ROWS - 2, HEAD), F32)
     tz[core, zl] = msg_f[...].astype(BF16)
 
+    stats[...] = jnp.zeros_like(stats)
+
     pl.semaphore_wait(barrier, PARTNERS)
 
     def table_z(target, sem):
@@ -124,17 +133,13 @@
         table_z((zl + p) % NZ, zl).start()
 
     def halo(h, which, step):
-        src, dst = ((k_hbm, k_buf), (v_hbm, v_buf))[which]
+        src = (k_hbm, v_hbm, q_hbm, g_hbm)[which]
+        dst = (k_buf, v_buf, query_in, grad_in)[which]
+        low, target = (MEM - step * SEG, seq_at(step)) if which < 2 else ((step - 1) * SEG, seq_at(-step))
         return remote(
-            src.at[:, columns(h)], dst.at[h, pl.ds(MEM - step * SEG, SEG)],
-            halo_s.at[which, step - 1, h], halo_r.at[which, step - 1, h], dp, seq_at(step),
+            src.at[:, columns(h)], dst.at[h, pl.ds(low, SEG)],
+            halo_s.at[which, step - 1, h], halo_r.at[which, step - 1, h], dp, target,
         )
-
-    @pl.loop(0, H)
-    def _(h):
-        for step in (1, 2):
-            for which in (0, 1):
-                halo(h, which, step).start()
 
     @pl.loop(1, NZ)
     def _(p):
@@ -143,6 +148,12 @@
 
     sib_table = remote(tz.at[core], tz.at[core], sib_s.at[0], sib_r.at[0], zl * 2 + other, seq)
     sib_table.start()
+
+    @pl.loop(0, H)
+    def _(i):
+        for which in (0, 1):
+            halo(turn(i, 1), which, 1).start()
+
     remote(tz.at[core], tz.at[other], sib_s.at[0], sib_r.at[0], zl * 2 + other, seq).wait_recv()
 
     for d in range(DP):
@@ -155,15 +166,20 @@
 
     @pl.loop(1, PLANE)
     def _(p):
-        table_plane(p, plane, (plane + p) % PLANE).start()
+        table_plane(p, plane, (plane - p + PLANE) % PLANE).start()
+
+    @pl.loop(0, H)
+    def _(i):
+        for which in (0, 1):
+            halo(turn(i, 2), which, 2).start()
+
+    @pl.loop(0, H)
+    def _(i):
+        for which in (2, 3):
+            halo(turn(i, -2), which, 2).start()
 
     load_q.wait()
     load_g.wait()
-
-    @pl.loop(1, PLANE)
-    def _(p):
-        source = (plane + p) % PLANE
-        table_plane(p, source, source).wait_recv()
 
     query_index = lax.broadcasted_iota(jnp.int32, (SEG, REL), 0)
     column_index = lax.broadcasted_iota(jnp.int32, (SEG, REL), 1)
@@ -172,29 +188,39 @@
         lax.broadcasted_iota(jnp.int32, (SEG, SEG), 0) + lax.broadcasted_iota(jnp.int32, (SEG, SEG), 1) == SEG - 1
     ).astype(F32).astype(BF16)
 
-    def give_back(h, which, step):
-        src, dst = ((back_k, got_k), (back_v, got_v))[which]
-        rows = pl.ds(MEM - step * SEG, SEG)
+    lane_index = lax.broadcasted_iota(jnp.int32, (SEG, HEAD), 1)
+    half_heads = H // 2
+
+    def with_biases(query, h):
+        biases = tz[h % 2, h // 2].astype(F32)
+        query = query.astype(F32)
+        return (query + biases[ROWS : ROWS + 1]).astype(BF16), (query + biases[ROWS + 1 : ROWS + 2]).astype(BF16)
+
+    def send_stats(group, step):
+        rows = pl.ds(group * STAT * half_heads, STAT * half_heads)
         return remote(
-            src.at[h, rows], dst.at[h, rows],
-            ret_s.at[which, step - 1, h], ret_r.at[which, step - 1, h], dp, seq_at(-step),
+            stats_out.at[rows], stats_in.at[step - 1, rows],
+            stat_s.at[group, step - 1], stat_r.at[group, step - 1], dp, seq_at(-step),
         )
 
     def send_tgrad(h):
         return remote(tgrad_out.at[h], tgrad_in.at[plane], tg_s.at[h], tg_r.at[plane], dp, plane_seq(h))
 
     @pl.loop(0, H)
-    def _(h):
+    def _(i):
+        h = turn(i, 0)
+
+        @pl.when(h != plane)
+        def _():
+            table_plane(0, h, h).wait_recv()
+
         for which in (0, 1):
             load_own(h, which).wait()
             for step in (1, 2):
                 halo(h, which, step).wait_recv()
         at = columns(h)
-        query = q_buf[:, at].astype(F32)
         grad = g_buf[:, at]
-        biases = tz[h % 2, h // 2].astype(F32)
-        content_query = (query + biases[ROWS : ROWS + 1]).astype(BF16)
-        position_query = (query + biases[ROWS + 1 : ROWS + 2]).astype(BF16)
+        content_query, position_query = with_biases(q_buf[:, at], h)
         keys = k_buf[h]
         values = v_buf[h]
         rows = table[h]
@@ -204,7 +230,8 @@
         scores = jnp.where(allowed, scores, -1e30)
         highest = jnp.max(scores, axis=1, keepdims=True)
         raised = jnp.where(allowed, jnp.exp(scores - highest), 0.0)
-        weights = raised * (1.0 / jnp.sum(raised, axis=1, keepdims=True))
+        inverse = 1.0 / jnp.sum(raised, axis=1, keepdims=True)
+        weights = raised * inverse
         rounded = weights.astype(BF16)
         att_ref[:, at] = dot_nn(rounded, values).astype(BF16)
         grad_probs = dot_nt(grad, values)
@@ -215,15 +242,28 @@
         grad_content = dot_nn(grad_scores, keys)
         grad_position = dot_nn(skewed, rows)
         qg_ref[:, at] = (grad_content + grad_position).astype(BF16)
-        key_part = dot_tn(grad_scores, content_query)
-        own_k[h] = key_part[MEM:]
-        back_k[h] = key_part[:MEM].astype(BF16)
-        value_part = dot_tn(rounded, grad)
-        own_v[h] = value_part[MEM:]
-        back_v[h] = value_part[:MEM].astype(BF16)
-        for step in (1, 2):
-            for which in (0, 1):
-                give_back(h, which, step).start()
+        own_k[h] = dot_tn(grad_scores[:, MEM:], content_query)
+        own_v[h] = dot_tn(rounded[:, MEM:], grad)
+        base = i * STAT
+        stats[...] = jnp.where(lane_index == base, highest, jnp.where(
+            lane_index == base + 1, inverse, jnp.where(lane_index == base + 2, mean, stats[...])))
+
+        for group in (0, 1):
+            @pl.when(i == half_heads * (group + 1) - 1)
+            def _():
+                flipped = stats[...].T
+                rows = slice(group * STAT * half_heads, (group + 1) * STAT * half_heads)
+                stats_out[rows] = flipped[rows]
+                for step in (1, 2):
+                    send_stats(group, step).start()
+
+        first, each = RELEASE
+        @pl.when((i >= first) & (i < first + H // each))
+        def _():
+            for j in range(each):
+                for which in (2, 3):
+                    halo(turn((i - first) * each + j, -1), which, 1).start()
+
         tgrad_out[h, :REL] = dot_tn(skewed, position_query).astype(BF16)
         content_sum = jnp.sum(grad_content, axis=0, keepdims=True)
         position_sum = jnp.sum(grad_position, axis=0, keepdims=True)
@@ -260,35 +300,104 @@
 
     sib_parts = remote(parts.at[other], sib_in, sib_s.at[1], sib_r.at[1], zl * 2 + other, seq)
     sib_parts.start()
-    sib_parts.wait_recv()
-    parts[core] += sib_in[...]
-
-    def send_half(target, slot):
-        return remote(parts.at[core, target], half_in.at[slot], half_s.at[target], half_r.at[slot], target * 2 + core, seq)
-
-    @pl.loop(1, NZ)
-    def _(p):
-        send_half((zl + p) % NZ, zl).start()
-
-    pair_out[...] = parts[core, zl]
-
-    @pl.loop(1, NZ)
-    def _(p):
-        source = (zl + p) % NZ
-        send_half(source, source).wait_recv()
-        pair_out[...] += half_in[source]
-
-    pair = remote(pair_out, pair_in, pair_s, pair_r, dp, plane * 2 + 1 - zh)
-    pair.start()
-    pair.wait_recv()
-    fin[plane] = pair_out[...] + pair_in[...]
+
+    def send_half(half, target, slot):
+        return remote(
+            half_out.at[target], half_in.at[slot], half_s.at[half, target], half_r.at[slot],
+            target * 2 + core, plane * 2 + half,
+        )
+
+    def along_z(act):
+        act(1 - zh, zl)
+
+        @pl.loop(1, NZ)
+        def _(p):
+            act(zh, (zl + p) % NZ)
+            act(1 - zh, (zl + p) % NZ)
 
     def send_fin(p, slot, target):
         return remote(fin.at[plane], fin.at[slot], fin_s.at[p], fin_r.at[slot], dp, plane_seq(target))
 
-    @pl.loop(1, PLANE)
-    def _(p):
-        send_fin(p, plane, (plane + p) % PLANE).start()
+    def take_stats(i, step):
+        for group in (0, 1):
+            @pl.when(i == half_heads * group)
+            def _():
+                send_stats(group, step).wait_recv()
+                lanes = slice(group * STAT * half_heads, (group + 1) * STAT * half_heads)
+                padded = jnp.concatenate([stats_in[step - 1, lanes]] * 2 + [
+                    jnp.zeros((SEG - 2 * STAT * half_heads, HEAD), F32)], axis=0)
+                stats_rows[step - 1] = padded.T
+
+    def later_part(h, step):
+        content_query, position_query = with_biases(query_in[h, (step - 1) * SEG : step * SEG], h)
+        grad = grad_in[h, (step - 1) * SEG : step * SEG]
+        rows = table[h, MEM - step * SEG : 2 * MEM - step * SEG]
+        positional = pltpu.roll(dot_nt(position_query, rows), SEG + 1, 1, stride=1, stride_axis=0)[:, :SEG]
+        scores = (dot_nt(content_query, k_buf[h, MEM:]) + positional) * factor
+        base = ((h - seq_at(step) // 2 + H) % H) * STAT
+        column = lambda at: jnp.sum(
+            jnp.where(lane_index == base + at, stats_rows[step - 1], 0.0), axis=1, keepdims=True)
+        weights = jnp.where(
+            lane_index < (32 - step - seq) * HEAD, jnp.exp(scores - column(0)) * column(1), 0.0)
+        grad_probs = dot_nt(grad, v_buf[h, MEM:])
+        grad_scores = (weights * (grad_probs - column(2)) * factor).astype(BF16)
+        return dot_tn(grad_scores, content_query), dot_tn(weights.astype(BF16), grad)
+
+    @pl.loop(0, H)
+    def _(i):
+        @pl.when(i == STAGES[0])
+        def _():
+            sib_parts.wait_recv()
+            parts[core] += sib_in[...]
+            low = lax.broadcasted_iota(jnp.int32, (MSG, HEAD), 0)
+
+            @pl.loop(0, NZ)
+            def _(p):
+                block = parts[core, p]
+                rest = block - block.astype(BF16).astype(F32)
+                block = jnp.where(low == ROWS + 2, rest[ROWS : ROWS + 1], jnp.where(
+                    low == ROWS + 3, rest[ROWS + 1 : ROWS + 2], block))
+                half_out[p] = block.astype(BF16)
+
+            along_z(lambda half, target: send_half(half, target, zh * NZ + zl).start())
+
+        h = turn(i, 2)
+        take_stats(i, 2)
+        for which in (2, 3):
+            halo(h, which, 2).wait_recv()
+        key_part, value_part = later_part(h, 2)
+        own_k[h] += key_part
+        own_v[h] += value_part
+
+    @pl.loop(0, H)
+    def _(i):
+        @pl.when(i == STAGES[1])
+        def _():
+            fin[plane] = half_out[zl].astype(F32)
+
+            def add(half, source):
+                slot = half * NZ + source
+                remote(half_out.at[source], half_in.at[slot], half_s.at[half, source], half_r.at[slot],
+                       source * 2 + core, plane * 2 + half).wait_recv()
+                fin[plane] += half_in[slot].astype(F32)
+
+            along_z(add)
+            total = fin[plane]
+            for r in range(ROWS):
+                fin[plane, r : r + 1] = total[ROWS - 1 - r : ROWS - r]
+
+            @pl.loop(1, PLANE)
+            def _(p):
+                send_fin(p, plane, (plane + p) % PLANE).start()
+
+        h = turn(i, 1)
+        take_stats(i, 1)
+        for which in (2, 3):
+            halo(h, which, 1).wait_recv()
+        key_part, value_part = later_part(h, 1)
+        at = columns(h)
+        kg_ref[:, at] = (own_k[h] + key_part).astype(BF16)
+        vg_ref[:, at] = (own_v[h] + value_part).astype(BF16)
 
     @pl.loop(1, PLANE)
     def _(p):
@@ -300,45 +409,38 @@
         tg_ref[:, columns(h)] = fin[h, :ROWS]
 
     mine = fin[dp]
-    cg_ref[...] = mine[ROWS : ROWS + 1]
-    pg_ref[...] = mine[ROWS + 1 : ROWS + 2]
-
-    @pl.loop(0, H)
-    def _(h):
-        for which in (0, 1):
-            for step in (1, 2):
-                give_back(h, which, step).wait_recv()
-        at = columns(h)
-        kg_ref[:, at] = (own_k[h] + got_k[h, :SEG].astype(F32) + got_k[h, SEG:].astype(F32)).astype(BF16)
-        vg_ref[:, at] = (own_v[h] + got_v[h, :SEG].astype(F32) + got_v[h, SEG:].astype(F32)).astype(BF16)
+    cg_ref[...] = mine[ROWS : ROWS + 1] + mine[ROWS + 2 : ROWS + 3]
+    pg_ref[...] = mine[ROWS + 1 : ROWS + 2] + mine[ROWS + 3 : ROWS + 4]
 
     sib_table.wait_send()
     sib_parts.wait_send()
-    pair.wait_send()
 
     @pl.loop(1, NZ)
     def _(p):
         target = (zl + p) % NZ
         table_z(target, zl).wait_send()
-        send_half(target, zl).wait_send()
 
     @pl.loop(1, PLANE)
     def _(p):
         target = (plane + p) % PLANE
-        table_plane(p, plane, target).wait_send()
+        table_plane(p, plane, (plane - p + PLANE) % PLANE).wait_send()
         send_fin(p, plane, target).wait_send()
         send_tgrad(target).wait_send()
 
+    along_z(lambda half, target: send_half(half, target, zh * NZ + zl).wait_send())
+    for step in (1, 2):
+        for group in (0, 1):
+            send_stats(group, step).wait_send()
+
     @pl.loop(0, H)
     def _(h):
         for step in (1, 2):
-            for which in (0, 1):
+            for which in range(4):
                 halo(h, which, step).wait_send()
-                give_back(h, which, step).wait_send()
 
 
 def local(queries, keys, values, position_keys, content_bias, position_bias, out_grad):
-    any_space = pl.BlockSpec(memory_space=pl.ANY)
+    hbm = pl.BlockSpec(memory_space=pltpu.HBM)
     vmem = pl.BlockSpec(memory_space=pltpu.VMEM)
     block = jax.ShapeDtypeStruct((SEG, HD), BF16)
     line = jax.ShapeDtypeStruct((1, HEAD), F32)
@@ -347,7 +449,7 @@
     attended, query_grad, key_grad, value_grad, table_grad, content_grad, position_grad = pl.pallas_call(
         kernel,
         out_shape=(block, block, block, block, jax.ShapeDtypeStruct((ROWS, HD), F32), line, line),
-        in_specs=[any_space] * 4 + [vmem] * 3,
+        in_specs=[hbm] * 4 + [vmem] * 3,
         out_specs=(vmem,) * 7,
         scratch_shapes=[
             pltpu.VMEM((SEG, HD), BF16),
@@ -358,8 +460,10 @@
             heads(SEG, F32),
             heads(MEM, BF16),
             heads(MEM, BF16),
-            heads(MEM, BF16),
-            heads(MEM, BF16),
+            pltpu.VMEM((SEG, HEAD), F32),
+            pltpu.VMEM((STAT * H, HEAD), F32),
+            pltpu.VMEM((2, STAT * H, HEAD), F32),
+            pltpu.VMEM((2, SEG, HEAD), F32),
             pltpu.VMEM((MSG, HEAD), F32),
             pltpu.VMEM((2, NZ, MSG, HEAD), BF16),
             pltpu.VMEM((REL, HEAD), F32),
@@ -368,16 +472,15 @@
             heads(TGRAD, BF16),
             pltpu.VMEM((2, NZ, MSG, HEAD), F32),
             pltpu.VMEM((NZ, MSG, HEAD), F32),
-            pltpu.VMEM((NZ, MSG, HEAD), F32),
-            pltpu.VMEM((MSG, HEAD), F32),
-            pltpu.VMEM((MSG, HEAD), F32),
+            pltpu.VMEM((NZ, MSG, HEAD), BF16),
+            pltpu.VMEM((2 * NZ, MSG, HEAD), BF16),
             heads(MSG, F32),
             dma((2,)),
             dma((2, H)),
-            dma((2, 2, H)),
-            dma((2, 2, H)),
-            dma((2, 2, H)),
-            dma((2, 2, H)),
+            dma((4, 2, H)),
+            dma((4, 2, H)),
+            dma((2, 2)),
+            dma((2, 2)),
             dma((NZ,)),
             dma((NZ,)),
             dma((2,)),
@@ -386,15 +489,13 @@
             dma((PLANE,)),
             dma((H,)),
             dma((PLANE,)),
-            dma((NZ,)),
-            dma((NZ,)),
-            dma,
-            dma,
+            dma((2, NZ)),
+            dma((2 * NZ,)),
             dma((PLANE,)),
             dma((PLANE,)),
         ],
         compiler_params=pltpu.CompilerParams(
-            collective_id=0, has_side_effects=True, vmem_limit_bytes=48 * 2**20
+            collective_id=0, has_side_effects=True, vmem_limit_bytes=60 * 2**20
         ),
     )(
         queries[0], keys[0], values[0], out_grad[0],
@@ -405,7 +506,7 @@
         query_grad[None],
         key_grad[None],
         value_grad[None],
-        jnp.flip(table_grad, axis=0),
+        table_grad,
         content_grad[0],
         position_grad[0],
     )

time: 300 us -> 251 us (0.84)
  Pallas kernels: 283 us -> 241 us
  local copies, waits for them, and re-layouts: 14.8 us -> 7.38 us
    pallas_call x1, Pallas kernels: 283 us -> 241 us  [local(): pl.pallas_call(kernel, out_shape=(block, block, block, block, jax.ShapeDt...]
    rev x1 -> x0, local copies, waits for them, and re-layouts: 4.86 us -> none  [local(): jnp.flip(table_grad, axis=0)]
    unnamed x20 -> x19, local copies, waits for them, and re-layouts: 9.9 us -> 7.38 us
where the time goes in v2:
time: 251 us; the launch traced here: 249 us
  Pallas kernels  241 us (96%)
  local copies, waits for them, and re-layouts  7.38 us (3%)
    pallas_call x1, Pallas kernels, local(): pl.pallas_call(kernel, out_shape=(block, block, block, block, jax.ShapeDt...  241 us
    unnamed x19, local copies, waits for them, and re-layouts  7.38 us

profile of v2, /device:TPU:6, one launch (start us, length us, event | category | flops | bytes accessed | tf_op | source)
XLA Modules:
  0.0 249.0 jit_solution(6874680127817261615)
XLA Ops:
  0.6 240.9 %shard_map.126 = (bf16[128,2048]{1,0:T(8,128)(2,1)}, bf16[128,2048]{1,0:T(8,128)(2,1)}, bf16[128,2048]{1,0:T(8,128)(2,1)}, bf16[128,2048]{1,0:T(8,128)(2,1)}, f3...) custom-call(bf16[128,2048]{1,0:T(8,128)(2,1)} %bitcast.16, bf16[128,2048]{1,0:T(8,128)(2,1)} %bitcast.17, ...), custom_call_target="tpu_custom_call" | custom-call | tf_op jit(solution)/shard_map/pallas_call | solution.py:449
  241.6 0.0 copy-start.2
  241.6 1.9 copy.21
  243.5 0.0 copy-done.2
  243.5 0.0 copy-start.1
  243.5 0.8 copy.22
  244.3 0.4 copy-done.1
  244.8 0.0 copy-start
  244.8 0.8 copy.23
  245.6 0.4 copy-done
  246.0 0.0 copy-start.3
  246.0 0.8 copy.24
  246.8 0.3 copy-done.3
  247.1 0.0 copy-start.5
  247.1 0.7 copy.25
  247.8 0.0 copy-done.5
  247.8 0.0 copy-start.4
  247.8 0.5 copy.26
  248.3 0.2 copy-done.4
  248.5 0.5 copy.27
Async XLA Ops:
  241.6 2.0 copy-start.2
  243.5 1.2 copy-start.1
  244.8 1.2 copy-start
  246.0 1.1 copy-start.3
  247.1 0.7 copy-start.5
  247.8 0.7 copy-start.4

commit v3 on v2

--- a/solution.py
+++ b/solution.py
@@ -20,8 +20,9 @@
 MSG = 32
 TGRAD = REL + 16
 STAT = 3
-STAGES = (1, 6)
-RELEASE = (4, 2)
+STAGES = (1, 2, 15)
+WINDOW = 10
+SPAN = 8
 PARTNERS = (PLANE - 1) + 2 * (NZ - 1) + 1 + 2
 
 F32 = jnp.float32
@@ -78,11 +79,9 @@
     load_q = pltpu.make_async_copy(q_hbm, q_buf, local_sem.at[0])
     load_g = pltpu.make_async_copy(g_hbm, g_buf, local_sem.at[1])
 
-    def load_own(h, which):
+    def load_own(which):
         src, dst = ((k_hbm, k_buf), (v_hbm, v_buf))[which]
-        return pltpu.make_async_copy(
-            src.at[:, columns(h)], dst.at[h, pl.ds(MEM, SEG)], own_sem.at[which, h]
-        )
+        return pltpu.make_async_copy(src, dst.at[pl.ds(MEM, SEG)], own_sem.at[which])
 
     barrier = pltpu.get_barrier_semaphore()
 
@@ -108,10 +107,8 @@
     load_q.start()
     load_g.start()
 
-    @pl.loop(0, H)
-    def _(i):
-        load_own(turn(i, 0), 0).start()
-        load_own(turn(i, 0), 1).start()
+    load_own(0).start()
+    load_own(1).start()
 
     rows_in = table_ref[:, columns(plane)].astype(F32)
     for r in range(ROWS):
@@ -137,7 +134,7 @@
         dst = (k_buf, v_buf, query_in, grad_in)[which]
         low, target = (MEM - step * SEG, seq_at(step)) if which < 2 else ((step - 1) * SEG, seq_at(-step))
         return remote(
-            src.at[:, columns(h)], dst.at[h, pl.ds(low, SEG)],
+            src.at[:, columns(h)], dst.at[pl.ds(low, SEG), columns(h)],
             halo_s.at[which, step - 1, h], halo_r.at[which, step - 1, h], dp, target,
         )
 
@@ -149,10 +146,30 @@
     sib_table = remote(tz.at[core], tz.at[core], sib_s.at[0], sib_r.at[0], zl * 2 + other, seq)
     sib_table.start()
 
-    @pl.loop(0, H)
-    def _(i):
-        for which in (0, 1):
-            halo(turn(i, 1), which, 1).start()
+    def beside(group, which):
+        src = (k_hbm, v_hbm, q_hbm, g_hbm)[which]
+        dst = (k_buf, v_buf, query_in, grad_in)[which]
+        low, target = (0, seq_at(2)) if which < 2 else (SEG, seq_at(-2))
+        at = pl.ds(pl.multiple_of(group * SPAN * HEAD, HEAD), SPAN * HEAD)
+        return remote(
+            src.at[:, at], dst.at[pl.ds(low, SEG), at],
+            halo_s.at[which, 1, group], halo_r.at[which, 1, group], dp, target,
+        )
+
+    def feed(n):
+        @pl.when(n < H)
+        def _():
+            for which in (0, 1):
+                halo(turn(n, 1), which, 1).start()
+
+        @pl.when((n >= H) & (n < 2 * H))
+        def _():
+            for which in (2, 3):
+                halo(turn(n - H, -1), which, 1).start()
+
+    @pl.loop(0, WINDOW)
+    def _(n):
+        feed(n)
 
     remote(tz.at[core], tz.at[other], sib_s.at[0], sib_r.at[0], zl * 2 + other, seq).wait_recv()
 
@@ -168,15 +185,15 @@
     def _(p):
         table_plane(p, plane, (plane - p + PLANE) % PLANE).start()
 
-    @pl.loop(0, H)
+    @pl.loop(0, H // SPAN)
     def _(i):
         for which in (0, 1):
-            halo(turn(i, 2), which, 2).start()
-
-    @pl.loop(0, H)
+            beside((turn(0, 2) // SPAN + i) % (H // SPAN), which).start()
+
+    @pl.loop(0, H // SPAN)
     def _(i):
         for which in (2, 3):
-            halo(turn(i, -2), which, 2).start()
+            beside((turn(0, -2) // SPAN + i) % (H // SPAN), which).start()
 
     load_q.wait()
     load_g.wait()
@@ -214,15 +231,26 @@
         def _():
             table_plane(0, h, h).wait_recv()
 
+        @pl.when(i == 0)
+        def _():
+            load_own(0).wait()
+            load_own(1).wait()
+
+        group = h // SPAN
+
+        @pl.when((i == 0) | ((h % SPAN == 0) & (group != plane // SPAN)))
+        def _():
+            for which in (0, 1):
+                beside(group, which).wait_recv()
+
         for which in (0, 1):
-            load_own(h, which).wait()
-            for step in (1, 2):
-                halo(h, which, step).wait_recv()
+            halo(h, which, 1).wait_recv()
+        feed(i + WINDOW)
         at = columns(h)
         grad = g_buf[:, at]
         content_query, position_query = with_biases(q_buf[:, at], h)
-        keys = k_buf[h]
-        values = v_buf[h]
+        keys = k_buf[:, at]
+        values = v_buf[:, at]
         rows = table[h]
         positional = pltpu.roll(dot_nt(position_query, rows), REL - SEG + 1, 1, stride=1, stride_axis=0)
         scores = (dot_nt(content_query, keys) + positional) * factor
@@ -257,13 +285,6 @@
                 for step in (1, 2):
                     send_stats(group, step).start()
 
-        first, each = RELEASE
-        @pl.when((i >= first) & (i < first + H // each))
-        def _():
-            for j in range(each):
-                for which in (2, 3):
-                    halo(turn((i - first) * each + j, -1), which, 1).start()
-
         tgrad_out[h, :REL] = dot_tn(skewed, position_query).astype(BF16)
         content_sum = jnp.sum(grad_content, axis=0, keepdims=True)
         position_sum = jnp.sum(grad_position, axis=0, keepdims=True)
@@ -278,28 +299,7 @@
         def _():
             send_tgrad(h).start()
 
-    flat[...] = tgrad_out[plane, :REL].astype(F32)
-    msg_f[0:16, :] = tgrad_out[plane, REL:].astype(F32)
-
-    @pl.loop(1, PLANE)
-    def _(p):
-        source = (plane + p) % PLANE
-        remote(tgrad_out.at[source], tgrad_in.at[source], tg_s.at[source], tg_r.at[source], dp, plane_seq(source)).wait_recv()
-        flat[...] += tgrad_in[source, :REL].astype(F32)
-        msg_f[0:16, :] += tgrad_in[source, REL:].astype(F32)
-
-    tail_rows = msg_f[0:16, :]
-    content_total = tail_rows[0:1] + tail_rows[1:2]
-    position_total = tail_rows[2:3] + tail_rows[3:4]
-    line = lax.broadcasted_iota(jnp.int32, (MSG - ROWS, HEAD), 0)
-    sums = jnp.where(line == 0, content_total, jnp.where(line == 1, position_total, 0.0))
-    for d in range(DP):
-        low = REL - ROWS * (d + 1)
-        parts[d % 2, d // 2, :ROWS] = flat[low : low + ROWS, :]
-        parts[d % 2, d // 2, ROWS:] = sums
-
     sib_parts = remote(parts.at[other], sib_in, sib_s.at[1], sib_r.at[1], zl * 2 + other, seq)
-    sib_parts.start()
 
     def send_half(half, target, slot):
         return remote(
@@ -318,34 +318,55 @@
     def send_fin(p, slot, target):
         return remote(fin.at[plane], fin.at[slot], fin_s.at[p], fin_r.at[slot], dp, plane_seq(target))
 
-    def take_stats(i, step):
-        for group in (0, 1):
-            @pl.when(i == half_heads * group)
-            def _():
-                send_stats(group, step).wait_recv()
-                lanes = slice(group * STAT * half_heads, (group + 1) * STAT * half_heads)
-                padded = jnp.concatenate([stats_in[step - 1, lanes]] * 2 + [
-                    jnp.zeros((SEG - 2 * STAT * half_heads, HEAD), F32)], axis=0)
-                stats_rows[step - 1] = padded.T
+    def take_stats(step, groups):
+        for group in groups:
+            send_stats(group, step).wait_recv()
+        width = STAT * half_heads
+        taken = [stats_in[step - 1, group * width : (group + 1) * width] for group in groups] * (3 - len(groups))
+        taken.append(jnp.zeros((SEG - 2 * width, HEAD), F32))
+        stats_rows[step - 1] = jnp.concatenate(taken, axis=0).T
 
     def later_part(h, step):
-        content_query, position_query = with_biases(query_in[h, (step - 1) * SEG : step * SEG], h)
-        grad = grad_in[h, (step - 1) * SEG : step * SEG]
+        content_query, position_query = with_biases(query_in[(step - 1) * SEG : step * SEG, columns(h)], h)
+        grad = grad_in[(step - 1) * SEG : step * SEG, columns(h)]
         rows = table[h, MEM - step * SEG : 2 * MEM - step * SEG]
         positional = pltpu.roll(dot_nt(position_query, rows), SEG + 1, 1, stride=1, stride_axis=0)[:, :SEG]
-        scores = (dot_nt(content_query, k_buf[h, MEM:]) + positional) * factor
+        scores = (dot_nt(content_query, k_buf[MEM:, columns(h)]) + positional) * factor
         base = ((h - seq_at(step) // 2 + H) % H) * STAT
         column = lambda at: jnp.sum(
             jnp.where(lane_index == base + at, stats_rows[step - 1], 0.0), axis=1, keepdims=True)
         weights = jnp.where(
             lane_index < (32 - step - seq) * HEAD, jnp.exp(scores - column(0)) * column(1), 0.0)
-        grad_probs = dot_nt(grad, v_buf[h, MEM:])
+        grad_probs = dot_nt(grad, v_buf[MEM:, columns(h)])
         grad_scores = (weights * (grad_probs - column(2)) * factor).astype(BF16)
         return dot_tn(grad_scores, content_query), dot_tn(weights.astype(BF16), grad)
 
     @pl.loop(0, H)
     def _(i):
         @pl.when(i == STAGES[0])
+        def _():
+            flat[...] = tgrad_out[plane, :REL].astype(F32)
+            msg_f[0:16, :] = tgrad_out[plane, REL:].astype(F32)
+
+            @pl.loop(1, PLANE)
+            def _(p):
+                source = (plane + p) % PLANE
+                remote(tgrad_out.at[source], tgrad_in.at[source], tg_s.at[source], tg_r.at[source], dp, plane_seq(source)).wait_recv()
+                flat[...] += tgrad_in[source, :REL].astype(F32)
+                msg_f[0:16, :] += tgrad_in[source, REL:].astype(F32)
+
+            tail_rows = msg_f[0:16, :]
+            content_total = tail_rows[0:1] + tail_rows[1:2]
+            position_total = tail_rows[2:3] + tail_rows[3:4]
+            line = lax.broadcasted_iota(jnp.int32, (MSG - ROWS, HEAD), 0)
+            sums = jnp.where(line == 0, content_total, jnp.where(line == 1, position_total, 0.0))
+            for d in range(DP):
+                low = REL - ROWS * (d + 1)
+                parts[d % 2, d // 2, :ROWS] = flat[low : low + ROWS, :]
+                parts[d % 2, d // 2, ROWS:] = sums
+            sib_parts.start()
+
+        @pl.when(i == STAGES[1])
         def _():
             sib_parts.wait_recv()
             parts[core] += sib_in[...]
@@ -361,17 +382,7 @@
 
             along_z(lambda half, target: send_half(half, target, zh * NZ + zl).start())
 
-        h = turn(i, 2)
-        take_stats(i, 2)
-        for which in (2, 3):
-            halo(h, which, 2).wait_recv()
-        key_part, value_part = later_part(h, 2)
-        own_k[h] += key_part
-        own_v[h] += value_part
-
-    @pl.loop(0, H)
-    def _(i):
-        @pl.when(i == STAGES[1])
+        @pl.when(i == STAGES[2])
         def _():
             fin[plane] = half_out[zl].astype(F32)
 
@@ -391,13 +402,28 @@
                 send_fin(p, plane, (plane + p) % PLANE).start()
 
         h = turn(i, 1)
-        take_stats(i, 1)
+        @pl.when(i == 0)
+        def _():
+            take_stats(1, (0,))
+            take_stats(2, (0, 1))
+
+            @pl.loop(0, H // SPAN)
+            def _(group):
+                for which in (2, 3):
+                    beside(group, which).wait_recv()
+
+        @pl.when(i == half_heads)
+        def _():
+            take_stats(1, (1,))
+
         for which in (2, 3):
             halo(h, which, 1).wait_recv()
-        key_part, value_part = later_part(h, 1)
+        feed(i + H + WINDOW)
+        key_near, value_near = later_part(h, 1)
+        key_far, value_far = later_part(h, 2)
         at = columns(h)
-        kg_ref[:, at] = (own_k[h] + key_part).astype(BF16)
-        vg_ref[:, at] = (own_v[h] + value_part).astype(BF16)
+        kg_ref[:, at] = (own_k[h] + key_near + key_far).astype(BF16)
+        vg_ref[:, at] = (own_v[h] + value_near + value_far).astype(BF16)
 
     @pl.loop(1, PLANE)
     def _(p):
@@ -434,9 +460,13 @@
 
     @pl.loop(0, H)
     def _(h):
-        for step in (1, 2):
-            for which in range(4):
-                halo(h, which, step).wait_send()
+        for which in range(4):
+            halo(h, which, 1).wait_send()
+
+    @pl.loop(0, H // SPAN)
+    def _(group):
+        for which in range(4):
+            beside(group, which).wait_send()
 
 
 def local(queries, keys, values, position_keys, content_bias, position_bias, out_grad):
@@ -454,12 +484,12 @@
         scratch_shapes=[
             pltpu.VMEM((SEG, HD), BF16),
             pltpu.VMEM((SEG, HD), BF16),
-            heads(REL, BF16),
-            heads(REL, BF16),
+            pltpu.VMEM((REL, HD), BF16),
+            pltpu.VMEM((REL, HD), BF16),
             heads(SEG, F32),
             heads(SEG, F32),
-            heads(MEM, BF16),
-            heads(MEM, BF16),
+            pltpu.VMEM((MEM, HD), BF16),
+            pltpu.VMEM((MEM, HD), BF16),
             pltpu.VMEM((SEG, HEAD), F32),
             pltpu.VMEM((STAT * H, HEAD), F32),
             pltpu.VMEM((2, STAT * H, HEAD), F32),
@@ -476,7 +506,7 @@
             pltpu.VMEM((2 * NZ, MSG, HEAD), BF16),
             heads(MSG, F32),
             dma((2,)),
-            dma((2, H)),
+            dma((2,)),
             dma((4, 2, H)),
             dma((4, 2, H)),
             dma((2, 2)),
@@ -495,7 +525,7 @@
             dma((PLANE,)),
         ],
         compiler_params=pltpu.CompilerParams(
-            collective_id=0, has_side_effects=True, vmem_limit_bytes=60 * 2**20
+            collective_id=0, has_side_effects=True, vmem_limit_bytes=52 * 2**20
         ),
     )(
         queries[0], keys[0], values[0], out_grad[0],

time: 251 us -> 241 us (0.960)
  Pallas kernels: 241 us -> 231 us
    pallas_call x1, Pallas kernels: 241 us -> 231 us  [local(): pl.pallas_call(kernel, out_shape=(block, block, block, block, jax.ShapeDt...]
    unnamed x19 -> x15, local copies, waits for them, and re-layouts: 7.38 us -> 6.86 us
where the time goes in v3:
time: 241 us; the launch traced here: 238 us
  Pallas kernels  231 us (96%)
  local copies, waits for them, and re-layouts  6.86 us (3%)
    pallas_call x1, Pallas kernels, local(): pl.pallas_call(kernel, out_shape=(block, block, block, block, jax.ShapeDt...  231 us
    unnamed x15, local copies, waits for them, and re-layouts  6.86 us

profile of v3, /device:TPU:6, one launch (start us, length us, event | category | flops | bytes accessed | tf_op | source)
XLA Modules:
  0.0 238.1 jit_solution(15380625825563835359)
XLA Ops:
  0.6 0.0 copy-start.1
  0.6 0.0 copy-start.2
  0.7 0.6 copy-done.1
  1.3 0.0 copy-done.2
  1.3 0.0 copy-start
  1.3 0.9 copy-done
  2.2 230.6 %shard_map.126 = (bf16[128,2048]{1,0:T(8,128)(2,1)S(1)}, bf16[128,2048]{1,0:T(8,128)(2,1)S(1)}, bf16[128,2048]{1,0:T(8,128)(2,1)S(1)}, bf16[128,2048]{1,0:T(8,12...) custom-call(bf16[128,2048]{1,0:T(8,128)(2,1)} %bitcast.20, ...), custom_call_target="tpu_custom_call" | custom-call | tf_op jit(solution)/shard_map/pallas_call | solution.py:479
  232.8 0.8 copy.21
  233.6 0.8 copy.22
  234.4 0.0 copy-start.3
  234.4 0.8 copy.23
  235.2 0.4 copy-done.3
  235.6 0.8 copy.24
  236.4 0.7 copy.25
  237.1 0.5 copy.26
  237.6 0.5 copy.27
Async XLA Ops:
  0.6 0.7 copy-start.1
  0.6 0.7 copy-start.2
  1.3 0.9 copy-start
  234.4 1.2 copy-start.3

commit v4 on v3

--- a/solution.py
+++ b/solution.py
@@ -20,7 +20,7 @@
 MSG = 32
 TGRAD = REL + 16
 STAT = 3
-STAGES = (1, 2, 15)
+STAGES = (1, 2, 14)
 WINDOW = 10
 SPAN = 8
 PARTNERS = (PLANE - 1) + 2 * (NZ - 1) + 1 + 2

time: 241 us -> 241 us (level)
  no operation moved by 1% of the time
where the time goes in v4:
time: 241 us; the launch traced here: 238 us
  Pallas kernels  231 us (96%)
  local copies, waits for them, and re-layouts  6.86 us (3%)
    pallas_call x1, Pallas kernels, local(): pl.pallas_call(kernel, out_shape=(block, block, block, block, jax.ShapeDt...  231 us
    unnamed x15, local copies, waits for them, and re-layouts  6.86 us

profile of v4, /device:TPU:6, one launch (start us, length us, event | category | flops | bytes accessed | tf_op | source)
XLA Modules:
  0.0 238.1 jit_solution(5131873481775173686)
XLA Ops:
  0.6 0.0 copy-start.1
  0.6 0.0 copy-start.2
  0.7 0.6 copy-done.1
  1.3 0.0 copy-done.2
  1.3 0.0 copy-start
  1.3 0.9 copy-done
  2.2 230.6 %shard_map.126 = (bf16[128,2048]{1,0:T(8,128)(2,1)S(1)}, bf16[128,2048]{1,0:T(8,128)(2,1)S(1)}, bf16[128,2048]{1,0:T(8,128)(2,1)S(1)}, bf16[128,2048]{1,0:T(8,12...) custom-call(bf16[128,2048]{1,0:T(8,128)(2,1)} %bitcast.20, ...), custom_call_target="tpu_custom_call" | custom-call | tf_op jit(solution)/shard_map/pallas_call | solution.py:479
  232.8 0.8 copy.21
  233.6 0.8 copy.22
  234.4 0.0 copy-start.3
  234.4 0.8 copy.23
  235.2 0.4 copy-done.3
  235.6 0.8 copy.24
  236.4 0.7 copy.25
  237.1 0.5 copy.26
  237.6 0.5 copy.27
Async XLA Ops:
  0.6 0.7 copy-start.1
  0.6 0.7 copy-start.2
  1.3 0.9 copy-start
  234.4 1.2 copy-start.3
